TPU v7x, 256 devices: a whole 4x4x8 slice. The times are simulated.
256 devices in a mesh: example: 64 (over x, z, core), feature: 4 (over y).
Axes of the slice: x: 4, y: 4, z: 8, core: 2. Of those that a mesh axis runs over, the one named last changes fastest.
Arguments:
- embeddings: bfloat16 [36864, 16384], P('example', 'feature'), may hold values from -16 to 16
- subspace: bfloat16 [16384, 128], P('feature'), may hold values from -0.046875 to 0.046875
- noise_levels: int32 [16384, 128], P('feature'), may hold values from -16 to 16
- targets: int32 [2048], replicated, may hold values from 0 to 16383
Outputs:
- embedding_grad: bfloat16 [36864, 16384], P('example', 'feature')
All inputs are finite; a program needn't handle non-finite values.
Results may differ from a plain program's by a relative error of at most 0.0085.
Values may be sent and summed in bfloat16 or wider, within the bound.
A program may use at most 64 MiB of HBM per device.

v0:
```python
import jax
import jax.numpy as jnp
from jax import lax
from jax.sharding import PartitionSpec as P

NOISE_STEP = 1.0 / 4096.0
HIGH = lax.Precision.HIGHEST


def transposed(former, latter, precision=None):
    return lax.dot_general(
        former,
        latter,
        (((0,), (0,)), ((), ())),
        precision=precision,
        preferred_element_type=jnp.float32,
    )


def by_columns(former, latter):
    return lax.dot_general(
        former, latter, (((1,), (1,)), ((), ())), preferred_element_type=jnp.float32
    )


def count_rows(targets, first, length):
    local = targets - first
    inside = (local >= 0) & (local < length)
    slots = jnp.where(inside, local, length)
    ones = jnp.ones(targets.shape, jnp.float32)
    return jax.ops.segment_sum(ones, slots, num_segments=length + 1)[:length]


def upper_factor(gram_matrix):
    return jnp.linalg.cholesky(gram_matrix).T


def factorize(gram_matrix):
    lower_factor = jnp.linalg.cholesky(gram_matrix)
    identity = jnp.eye(gram_matrix.shape[0], dtype=jnp.float32)
    inverse_factor = jax.scipy.linalg.solve_triangular(lower_factor, identity, lower=True)
    gram_inverse = jnp.dot(inverse_factor.T, inverse_factor, precision=HIGH)
    return (inverse_factor, gram_inverse)


def on_device(embeddings, subspace, noise_levels, targets):
    row_count, local_width = embeddings.shape
    examples = lax.axis_size("example")
    total_rows = row_count * examples
    projected = lax.psum(
        jnp.dot(embeddings, subspace, preferred_element_type=jnp.float32), "feature"
    )
    projected_low = projected.astype(jnp.bfloat16)
    feature_first = lax.axis_index("feature") * local_width
    share = local_width // examples
    summed = lax.psum_scatter(
        transposed(embeddings, projected_low), "example", scatter_dimension=0, tiled=True
    )
    offset = lax.axis_index("example") * share
    noise_part = lax.dynamic_slice_in_dim(noise_levels, offset, share, 0)
    image = summed / total_rows + NOISE_STEP * noise_part.astype(jnp.float32)
    row_counts = count_rows(targets, feature_first + offset, share)
    gram_matrix = lax.psum(transposed(image, image, HIGH), ("example", "feature"))
    inverse_factor, gram_inverse = factorize(gram_matrix)
    orthonormal = jnp.dot(image, inverse_factor.T, precision=HIGH)
    alignment = lax.psum(
        transposed(orthonormal * row_counts[:, None], orthonormal, HIGH), ("example", "feature")
    )
    factor_grad = 2.0 * jnp.dot(alignment, inverse_factor, precision=HIGH)
    unused, pull_back = jax.vjp(upper_factor, gram_matrix)
    gram_grad = pull_back(factor_grad)[0]
    image_grad = jnp.dot(image, gram_grad + gram_grad.T, precision=HIGH) - 2.0 * row_counts[
        :, None
    ] * jnp.dot(image, gram_inverse, precision=HIGH)
    grad_low = image_grad.astype(jnp.bfloat16)
    grad_low = lax.all_gather(grad_low, "example", axis=0, tiled=True)
    back_sum = lax.psum(
        jnp.dot(embeddings, grad_low, preferred_element_type=jnp.float32), "feature"
    )
    back_rows = back_sum.astype(jnp.bfloat16)
    result = by_columns(projected_low, grad_low) + by_columns(back_rows, subspace)
    return result.astype(jnp.bfloat16)


def solution(mesh):
    in_specs = (P("example", "feature"), P("feature", None), P("feature", None), P())
    out_specs = P("example", "feature")
    return jax.shard_map(
        on_device, mesh=mesh, in_specs=in_specs, out_specs=out_specs, check_vma=False
    )
```

profile of v0, /device:TPU:2, one launch (start us, length us, event | category | flops | bytes accessed | tf_op | source)
XLA Modules:
  0.0 797.7 jit_solution(3288870860719686440)
XLA Ops:
  6.5 0.0 copy-start
  6.5 0.0 reduce-scatter.4.cloned.1.call-start
  6.5 4.2 fusion.45
  10.7 20.2 %all-reduce.8 = bf16[576,128]{1,0:T(8,128)(2,1)S(1)} all-reduce(f32[576,128]{1,0:T(8,128)S(1)} %fusion.45), channel_id=1, replica_groups=mesh['example'=64,'feature'=4] {'feature'}, use_global_device_ids=true, to_apply=%region_0.0 | all-reduce | flops 73728 | bytes 442368 | tf_op jit(solution)/shard_map/psum | solution.py:50
  30.9 4.7 convolution_bitcast_fusion
  35.6 0.0 copy-start.3
  35.6 2.9 copy.14
  38.5 0.0 reduce-scatter.4.cloned.1.call-update
  38.6 0.0 all-reduce.5.cloned.1.call-start
  38.6 0.0 copy-done
  38.6 0.1 copy.16
  38.7 0.0 copy-done.3
  38.8 14.7 %scatter_custom_fusion = f32[65]{0:T(128)S(1)} fusion(s32[2048]{0:T(1024)S(1)} %and_select_fusion, f32[2048]{0:T(1024)S(1)} %broadcast.95, f32[]{:T(128)} %constant.76.clone.1), kind=kCustom, calls=%fused_computation.59 | custom fusion | flops 2048 | bytes 264 | tf_op jit(solution)/shard_map/scatter-add | solution.py:31
  53.5 126.3 %reduce-scatter.4.cloned.1.call-done = f32[64,128]{1,0:T(8,128)} async-done(((f32[4096,128]{1,0:T(8,128)}), f32[64,128]{1,0:T(8,128)}) %reduce-scatter.4.cloned.1.call-update) | async-done | bytes 32784
  179.7 0.8 copy.15
  180.6 0.9 fusion.46
  181.5 0.0 all-reduce.5.cloned.1.call-update
  181.5 0.0 all-reduce.7.cloned.1.call-start
  181.6 240.4 %all-reduce.5.cloned.1.call-done = f32[128,128]{0,1:T(8,128)} async-done(((f32[128,128]{0,1:T(8,128)}), f32[128,128]{0,1:T(8,128)}) %all-reduce.5.cloned.1.call-update) | async-done | bytes 65552 | tf_op jit(solution)/shard_map/psum | solution.py:63
  422.0 0.9 copy.11
  423.0 0.9 fusion.22
  423.8 11.7 %custom-call.14 = f32[128,128]{1,0:T(8,128)S(1)} custom-call(f32[128,128]{1,0:T(8,128)S(1)} %fusion.22), custom_call_target="Cholesky" | custom-call | tf_op jit(solution)/shard_map/jvp(jit(cholesky))/cholesky/custom-call.1 | solution.py:35
  435.6 0.7 compare_reduce_fusion
  436.2 0.6 fusion.24
  436.9 9.8 %custom-call.13 = f32[1,128,128]{1,2,0:T(8,128)S(1)} custom-call(f32[1,128,128]{2,1,0:T(8,128)S(1)} %fusion.24), custom_call_target="InvertDiagBlocksLowerTriangular" | custom-call | tf_op jit(solution)/shard_map/transpose(jvp(jit(cholesky)))/triangular_solve | solution.py:35
  446.7 0.2 fusion.20
  446.9 0.3 fusion.47
  447.2 1.0 fusion.29
  448.2 0.0 all-reduce.7.cloned.1.call-update
  448.2 0.2 all-gather.2.cloned.1.call-start
  448.5 0.3 fusion.48
  448.7 233.9 %all-reduce.7.cloned.1.call-done = f32[128,128]{1,0:T(8,128)} async-done(((f32[128,128]{1,0:T(8,128)}), f32[128,128]{1,0:T(8,128)}) %all-reduce.7.cloned.1.call-update) | async-done | bytes 65552 | tf_op jit(solution)/shard_map/psum | solution.py:66
  682.6 1.1 fusion.1
  683.7 0.9 fusion
  684.6 0.2 fusion.18
  684.9 0.3 fusion.16
  685.1 0.1 copy.12
  685.2 0.3 fusion.12
  685.5 0.9 fusion.3
  686.4 0.0 all-gather.2.cloned.1.call-update
  686.4 72.9 %all-gather.2.cloned.1.call-done = bf16[4096,128]{1,0:T(8,128)(2,1)} async-done(((bf16[64,128]{1,0:T(8,128)(2,1)}), bf16[4096,128]{1,0:T(8,128)(2,1)}) %all-gather.2.cloned.1.call-update) | async-done | bytes 1048592 | tf_op jit(solution)/shard_map/all_gather | solution.py:76
  759.3 0.0 copy-start.1
  759.3 5.2 convolution_bitcast_fusion.1
  764.5 21.6 %all-reduce.9 = bf16[576,128]{0,1:T(8,128)(2,1)S(1)} all-reduce(f32[576,128]{0,1:T(8,128)} %convolution_bitcast_fusion.1), channel_id=1, replica_groups=mesh['example'=64,'feature'=4] {'feature'}, use_global_device_ids=true, to_apply=%region_7.9 | all-reduce | flops 73728 | bytes 442368 | tf_op jit(solution)/shard_map/psum | solution.py:77
  786.1 0.0 copy-done.1
  786.1 0.0 copy-start.2
  786.1 1.4 fusion.49
  787.5 0.0 copy-done.2
  787.5 3.6 add_convert_fusion
  (7 shorter events, 0.1 us)
Async XLA Ops:
  6.5 32.1 %copy-start = (s32[4096,128]{1,0:T(8,128)S(1)}, s32[4096,128]{1,0:T(8,128)}, u32[]{:S(2)}) copy-start(s32[4096,128]{1,0:T(8,128)} %param.7) | copy-start | bytes 6291460
  6.5 173.2 %reduce-scatter.4.cloned.1.call-start = ((), (), s32[]{:S(2)}) async-start(), calls=%async_computation.4 | async-start | bytes 2129920
  35.6 3.2 copy-start.3
  38.6 383.5 %all-reduce.5.cloned.1.call-start = ((), (), s32[]{:S(2)}) async-start(), calls=%async_computation.1 | async-start | bytes 131072 | tf_op jit(solution)/shard_map/psum | solution.py:63
  181.5 501.1 %all-reduce.7.cloned.1.call-start = ((), (), s32[]{:S(2)}) async-start(), calls=%async_computation.2 | async-start | bytes 131072 | tf_op jit(solution)/shard_map/psum | solution.py:66
  448.2 311.1 %all-gather.2.cloned.1.call-start = ((), (), s32[]{:S(2)}) async-start(), calls=%async_computation.3 | async-start | bytes 1064960 | tf_op jit(solution)/shard_map/all_gather | solution.py:76
  759.3 26.8 %copy-start.1 = (bf16[4096,128]{1,0:T(8,128)(2,1)S(1)}, bf16[4096,128]{1,0:T(8,128)(2,1)}, u32[]{:S(2)}) copy-start(bf16[4096,128]{1,0:T(8,128)(2,1)} %all-gather.2.cloned.1.call-done) | copy-start | bytes 3145732
  786.1 1.4 copy-start.2
Sparse Core Ops, SparseCore 0:
  38.7 140.9 reduce-scatter.3
  186.1 235.8 all-reduce.4
  448.3 234.2 all-reduce.6
  686.6 72.6 all-gather.1
where the time goes:
time: 798 us
  waiting for transfers between devices  674 us (84%)
  blocking collectives  41.8 us (5%)
  other arithmetic  38.4 us (5%)
  matrix products  25.4 us (3%)
  between operations  13.3 us (2%)
    psum x1, waiting for transfers between devices, on_device(): lax.psum(transposed(image, image, HIGH), ('example', 'feature'))  240 us
    psum x1, waiting for transfers between devices, on_device(): lax.psum(transposed(orthonormal * row_counts[:, None], orthonormal, HIGH)...  234 us
    unnamed x5, waiting for transfers between devices  126 us
    all_gather x1, waiting for transfers between devices, on_device(): grad_low = lax.all_gather(grad_low, 'example', axis=0, tiled=True)  72.9 us
    another operation x5, other arithmetic, upper_factor(): return jnp.linalg.cholesky(gram_matrix).T  22.8 us
    psum x1, blocking collectives, on_device(): lax.psum(jnp.dot(embeddings, grad_low, preferred_element_type=jnp.float32...  21.6 us
    psum x1, blocking collectives, on_device(): lax.psum(jnp.dot(embeddings, subspace, preferred_element_type=jnp.float32...  20.2 us
  transfers between devices with their start and end apart: 4, of which 4 were waited for; matrix products, arithmetic and copies ran while one was open for 2% of the time, Pallas kernels for 0%

commit v1 on v0

--- a/solution.py
+++ b/solution.py
@@ -5,6 +5,14 @@
 
 NOISE_STEP = 1.0 / 4096.0
 HIGH = lax.Precision.HIGHEST
+
+
+def gather_by_exchange(array, axis, dim):
+    length = lax.axis_size(axis)
+    repeats = [length if d == dim else 1 for d in range(array.ndim)]
+    return lax.all_to_all(
+        jnp.tile(array, repeats), axis, split_axis=dim, concat_axis=dim, tiled=True
+    )
 
 
 def transposed(former, latter, precision=None):
@@ -73,7 +81,7 @@
         :, None
     ] * jnp.dot(image, gram_inverse, precision=HIGH)
     grad_low = image_grad.astype(jnp.bfloat16)
-    grad_low = lax.all_gather(grad_low, "example", axis=0, tiled=True)
+    grad_low = gather_by_exchange(grad_low, "example", 0)
     back_sum = lax.psum(
         jnp.dot(embeddings, grad_low, preferred_element_type=jnp.float32), "feature"
     )

time: 798 us -> 765 us (0.959)
  waiting for transfers between devices: 674 us -> 601 us
  blocking collectives: 41.8 us -> 75 us
    all_gather x1 -> x0, waiting for transfers between devices: 72.9 us -> none  [on_device(): grad_low = lax.all_gather(grad_low, 'example', axis=0, tiled=True)]
    all_to_all x0 -> x1, blocking collectives: none -> 33.8 us  [gather_by_exchange(): lax.all_to_all(jnp.tile(array, repeats), axis, split_axis=dim, concat_axi...]
    unnamed x5 -> x4, waiting for transfers between devices: 126 us -> 126 us
  transfers between devices with their start and end apart: 4 -> 3, of which waited for: 4 -> 3; matrix products, arithmetic and copies ran while one was open for 2% -> 2% of each run, Pallas kernels for 0% -> 0%
where the time goes in v1:
time: 765 us; the launch traced here: 764 us
  waiting for transfers between devices  601 us (79%)
  blocking collectives  75 us (10%)
  other arithmetic  38.4 us (5%)
  matrix products  31.4 us (4%)
  between operations  13.3 us (2%)
    psum x1, waiting for transfers between devices, on_device(): lax.psum(transposed(image, image, HIGH), ('example', 'feature'))  240 us
    psum x1, waiting for transfers between devices, on_device(): lax.psum(transposed(orthonormal * row_counts[:, None], orthonormal, HIGH)...  234 us
    unnamed x4, waiting for transfers between devices  126 us
    all_to_all x1, blocking collectives, gather_by_exchange(): lax.all_to_all(jnp.tile(array, repeats), axis, split_axis=dim, concat_axi...  33.8 us
    another operation x5, other arithmetic, upper_factor(): return jnp.linalg.cholesky(gram_matrix).T  22.8 us
    psum x1, blocking collectives, on_device(): lax.psum(jnp.dot(embeddings, grad_low, preferred_element_type=jnp.float32...  21.1 us
    psum x1, blocking collectives, on_device(): lax.psum(jnp.dot(embeddings, subspace, preferred_element_type=jnp.float32...  20.2 us
  transfers between devices with their start and end apart: 3, of which 3 were waited for; matrix products, arithmetic and copies ran while one was open for 2% of the time, Pallas kernels for 0%

profile of v1, /device:TPU:2, one launch (start us, length us, event | category | flops | bytes accessed | tf_op | source)
XLA Modules:
  0.0 764.2 jit_solution(2596139925950020157)
XLA Ops:
  6.5 0.0 copy-start
  6.5 0.0 reduce-scatter.4.cloned.1.call-start
  6.5 4.2 fusion.45
  10.7 20.2 %all-reduce.8 = bf16[576,128]{1,0:T(8,128)(2,1)S(1)} all-reduce(f32[576,128]{1,0:T(8,128)S(1)} %fusion.45), channel_id=1, replica_groups=mesh['example'=64,'feature'=4] {'feature'}, use_global_device_ids=true, to_apply=%region_0.0 | all-reduce | flops 73728 | bytes 442368 | tf_op jit(solution)/shard_map/psum | solution.py:58
  30.9 4.7 convolution_bitcast_fusion
  35.6 0.0 copy-start.1
  35.6 2.9 copy.14
  38.5 0.0 reduce-scatter.4.cloned.1.call-update
  38.6 0.0 all-reduce.5.cloned.1.call-start
  38.6 0.0 copy-done
  38.6 0.1 copy.16
  38.7 0.0 copy-done.1
  38.8 14.7 %scatter_custom_fusion = f32[65]{0:T(128)S(1)} fusion(s32[2048]{0:T(1024)S(1)} %and_select_fusion, f32[2048]{0:T(1024)S(1)} %broadcast.98, f32[]{:T(128)} %constant.76.clone.1), kind=kCustom, calls=%fused_computation.59 | custom fusion | flops 2048 | bytes 264 | tf_op jit(solution)/shard_map/scatter-add | solution.py:39
  53.5 126.3 %reduce-scatter.4.cloned.1.call-done = f32[64,128]{1,0:T(8,128)} async-done(((f32[4096,128]{1,0:T(8,128)}), f32[64,128]{1,0:T(8,128)}) %reduce-scatter.4.cloned.1.call-update) | async-done | bytes 32784
  179.7 0.8 copy.15
  180.6 0.9 fusion.46
  181.5 0.0 all-reduce.5.cloned.1.call-update
  181.5 0.2 all-reduce.7.cloned.1.call-start
  181.8 240.3 %all-reduce.5.cloned.1.call-done = f32[128,128]{0,1:T(8,128)} async-done(((f32[128,128]{0,1:T(8,128)}), f32[128,128]{0,1:T(8,128)}) %all-reduce.5.cloned.1.call-update) | async-done | bytes 65552 | tf_op jit(solution)/shard_map/psum | solution.py:71
  422.0 0.9 copy.11
  423.0 0.9 fusion.22
  423.8 11.7 %custom-call.14 = f32[128,128]{1,0:T(8,128)S(1)} custom-call(f32[128,128]{1,0:T(8,128)S(1)} %fusion.22), custom_call_target="Cholesky" | custom-call | tf_op jit(solution)/shard_map/jvp(jit(cholesky))/cholesky/custom-call.1 | solution.py:43
  435.6 0.7 compare_reduce_fusion
  436.2 0.6 fusion.24
  436.9 9.8 %custom-call.13 = f32[1,128,128]{1,2,0:T(8,128)S(1)} custom-call(f32[1,128,128]{2,1,0:T(8,128)S(1)} %fusion.24), custom_call_target="InvertDiagBlocksLowerTriangular" | custom-call | tf_op jit(solution)/shard_map/transpose(jvp(jit(cholesky)))/triangular_solve | solution.py:43
  446.7 0.2 fusion.20
  446.9 0.3 fusion.47
  447.2 1.0 fusion.29
  448.2 0.0 all-reduce.7.cloned.1.call-update
  448.2 0.3 fusion.48
  448.5 234.1 %all-reduce.7.cloned.1.call-done = f32[128,128]{1,0:T(8,128)} async-done(((f32[128,128]{1,0:T(8,128)}), f32[128,128]{1,0:T(8,128)}) %all-reduce.7.cloned.1.call-update) | async-done | bytes 65552 | tf_op jit(solution)/shard_map/psum | solution.py:74
  682.6 1.1 fusion.1
  683.7 0.9 fusion
  684.6 0.2 fusion.18
  684.9 0.3 fusion.16
  685.1 0.1 copy.12
  685.2 0.3 fusion.12
  685.5 0.3 fusion.3
  685.8 0.2 tile.2
  686.1 33.8 %all_to_all.9 = bf16[64,64,128]{2,1,0:T(8,128)(2,1)S(1)} all-to-all(bf16[64,64,128]{2,1,0:T(8,128)(2,1)S(1)} %tile.2), channel_id=1, replica_groups=mesh['example'=64,'feature'=4] {'example'}, dimensions={0} | all-to-all | bytes 2097152 | tf_op jit(solution)/shard_map/all_to_all | solution.py:13
  719.8 4.1 convolution_bitcast_fusion.1
  724.0 5.0 fusion.49
  729.0 21.1 %all-reduce.9 = bf16[576,128]{0,1:T(8,128)(2,1)S(1)} all-reduce(f32[576,128]{0,1:T(8,128)S(1)} %convolution_bitcast_fusion.1), channel_id=1, replica_groups=mesh['example'=64,'feature'=4] {'feature'}, use_global_device_ids=true, to_apply=%region_7.9 | all-reduce | flops 73728 | bytes 442368 | tf_op jit(solution)/shard_map/psum | solution.py:85
  750.1 7.6 add_convert_fusion
  (7 shorter events, 0.1 us)
Async XLA Ops:
  6.5 32.1 %copy-start = (s32[4096,128]{1,0:T(8,128)S(1)}, s32[4096,128]{1,0:T(8,128)}, u32[]{:S(2)}) copy-start(s32[4096,128]{1,0:T(8,128)} %param.7) | copy-start | bytes 6291460
  6.5 173.2 %reduce-scatter.4.cloned.1.call-start = ((), (), s32[]{:S(2)}) async-start(), calls=%async_computation.4 | async-start | bytes 2129920
  35.6 3.2 copy-start.1
  38.6 383.5 %all-reduce.5.cloned.1.call-start = ((), (), s32[]{:S(2)}) async-start(), calls=%async_computation.2 | async-start | bytes 131072 | tf_op jit(solution)/shard_map/psum | solution.py:71
  181.5 501.1 %all-reduce.7.cloned.1.call-start = ((), (), s32[]{:S(2)}) async-start(), calls=%async_computation.3 | async-start | bytes 131072 | tf_op jit(solution)/shard_map/psum | solution.py:74
Sparse Core Ops, SparseCore 0:
  38.7 140.9 reduce-scatter.3
  186.1 235.8 all-reduce.4
  448.3 234.2 all-reduce.6
